TPU v7x, 32 devices: a whole 2x2x4 slice. The times are simulated.
32 devices in a mesh: groups: 2 (over x), ctx: 8 (over z, y), head: 2 (over core).
Axes of the slice: x: 2, y: 2, z: 4, core: 2. Of those that a mesh axis runs over, the one named last changes fastest.
Arguments:
- queries: bfloat16 [4096, 20, 128], P(('groups', 'ctx'), 'head'), parts along dimension 0, may hold values from -70 to 70, as said below
- keys: bfloat16 [4096, 4, 128], P(('groups', 'ctx'), 'head'), parts along dimension 0, may hold values from -3.5 to 3.5
- doc_lengths: int32 [8], P('groups'), parts along dimension 0, may hold values from 1 to 24, 32 in all
- gate_query_weight: bfloat16 [20, 128, 128], P('head'), may hold values from -0.5 to 0.5
- gate_key_weight: bfloat16 [4, 384, 128], P('head'), may hold values from -0.3125 to 0.3125
Outputs:
- block_targets: float32 [20, 64, 32], P('head', ('groups', 'ctx')), parts along dimension 1
- key_proj_grad: float32 [64, 4, 128], P(('groups', 'ctx'), 'head'), parts along dimension 0
- query_weight_grad: float32 [40, 128, 128], P(('groups', 'head')), parts along dimension 0
- key_weight_grad: float32 [8, 384, 128], P(('groups', 'head')), parts along dimension 0
There are 2 independent parts, one for each index of `groups`. A program takes and returns all parts, laid end to end along the dimension named above; an argument that names none is the same for every part. Nothing has to cross between parts.
Inputs may be any that keep to these rules, and one draw needn't show every extreme that they name: queries are of order one except in a few rows.
All inputs are finite; a program needn't handle non-finite values.
Results may differ from a plain program's by a relative error of at most 0.006.
Values may be sent and summed in bfloat16 or wider, within the bound.
No kernel may reach another device: no remote copies, remote signals or barrier semaphores. Data moves between devices by JAX's collectives and lax.ppermute only.
A program may use at most 64 MiB of HBM per device.

v0:
```python
import math

import jax
import jax.numpy as jnp
from jax import lax
from jax.sharding import PartitionSpec as P

BLK = 64


def absorb(state, query_group, positions, lowest, key_piece, piece_start, score_scale):
    group_rows, local_kv, repeats, head_size = query_group.shape
    local_heads = local_kv * repeats
    piece_rows = key_piece.shape[0]
    tile_width = 512
    key_tiles = key_piece.reshape(piece_rows // tile_width, tile_width, local_kv, head_size)
    tile_offsets = jnp.arange(piece_rows // tile_width, dtype=jnp.int32) * tile_width

    def one_tile(carried, tile_item):
        running_max, running_sum, block_best = carried
        key_tile, tile_offset = tile_item
        scores = jnp.einsum(
            "rgfd,ngd->gfrn", query_group, key_tile, preferred_element_type=jnp.float32
        )
        scores = scores.reshape(local_heads, group_rows, tile_width) * score_scale
        key_positions = tile_offset + jnp.arange(tile_width, dtype=jnp.int32)
        allowed = (key_positions[None, :] <= positions[:, None]) & (
            key_positions[None, :] >= lowest[:, None]
        )
        scores = jnp.where(allowed[None], scores, -1e30)
        new_max = jnp.maximum(running_max, jnp.max(scores, axis=-1))
        weights = jnp.where(allowed[None], jnp.exp(scores - new_max[..., None]), 0.0)
        running_sum = running_sum * jnp.exp(running_max - new_max) + jnp.sum(weights, axis=-1)
        tile_best = jnp.max(
            scores.reshape(local_heads, group_rows, tile_width // BLK, BLK), axis=-1
        )
        block_best = lax.dynamic_update_slice(
            block_best, tile_best, (jnp.int32(0), jnp.int32(0), tile_offset // BLK)
        )
        return ((new_max, running_sum, block_best), None)

    def do_work(carried):
        return lax.scan(one_tile, carried, (key_tiles, tile_offsets))[0]

    def keep_state(carried):
        return carried

    needed = (piece_start <= positions[-1]) & (piece_start + piece_rows > lowest[0])
    return lax.cond(needed, do_work, keep_state, state)


def finish(state, query_group, group_start, doc_start, all_key_proj, gate_query_weight, gate_scale):
    running_max, running_sum, block_best = state
    local_heads, group_rows, block_count = block_best.shape
    group_rows_q, local_kv, repeats, head_size = query_group.shape
    gate_size = gate_query_weight.shape[2]
    group_blocks = group_rows // BLK
    log_total = running_max + jnp.log(running_sum)
    ratios = (
        jnp.exp(block_best - log_total[..., None])
        .reshape(local_heads, group_blocks, BLK, block_count)
        .max(2)
    )
    query_blocks = group_start // BLK + jnp.arange(group_blocks, dtype=jnp.int32)
    key_block_ids = jnp.arange(block_count, dtype=jnp.int32)
    block_mask = (key_block_ids[None, :] <= query_blocks[:, None]) & (
        key_block_ids[None, :] >= doc_start[query_blocks][:, None]
    )
    ratios = jnp.where(block_mask[None], ratios, 0.0)
    targets = ratios / jnp.sum(ratios, axis=-1, keepdims=True)
    pooled_queries = (
        query_group.reshape(group_blocks, BLK, local_heads, head_size)
        .astype(jnp.float32)
        .mean(1)
        .astype(jnp.bfloat16)
    )
    query_proj = jnp.einsum(
        "ahd,hde->ahe", pooled_queries, gate_query_weight, preferred_element_type=jnp.float32
    )
    proj_split = query_proj.reshape(group_blocks, local_kv, repeats, gate_size)
    logits = jnp.einsum("agre,cge->grac", proj_split, all_key_proj, precision=lax.Precision.HIGHEST)
    logits = logits.reshape(local_heads, group_blocks, block_count) * gate_scale
    logits = jnp.where(block_mask[None], logits, -1e30)
    gate_exp = jnp.exp(logits - jnp.max(logits, axis=-1, keepdims=True))
    gate_probs = gate_exp / jnp.sum(gate_exp, axis=-1, keepdims=True)
    delta = jnp.where(block_mask[None], gate_probs - targets, 0.0)
    delta_split = delta.reshape(local_kv, repeats, group_blocks, block_count)
    query_grad = jnp.einsum(
        "grac,cge->agre", delta_split, all_key_proj, precision=lax.Precision.HIGHEST
    )
    query_grad = query_grad.reshape(group_blocks, local_heads, gate_size) * gate_scale
    key_grad = (
        jnp.einsum("grac,agre->cge", delta_split, proj_split, precision=lax.Precision.HIGHEST)
        * gate_scale
    )
    return (targets, pooled_queries, query_grad, key_grad)


def per_device(queries, keys, doc_lengths, gate_query_weight, gate_key_weight):
    local_rows, local_heads, head_size = queries.shape
    local_kv = keys.shape[1]
    repeats = local_heads // local_kv
    ctx_count = lax.axis_size("ctx")
    ctx_rank = lax.axis_index("ctx")
    local_blocks = local_rows // BLK
    block_count = local_blocks * ctx_count
    half_rows = local_rows // 2
    score_scale = 1.0 / math.sqrt(head_size)
    gate_scale = 1.0 / math.sqrt(gate_query_weight.shape[2])
    doc_ends = jnp.cumsum(doc_lengths)
    doc_begins = doc_ends - doc_lengths
    block_ids = jnp.arange(block_count, dtype=jnp.int32)
    doc_start = jnp.max(
        jnp.where(doc_begins[None, :] <= block_ids[:, None], doc_begins[None, :], 0), axis=1
    )
    key_blocks = keys.reshape(local_blocks, BLK, local_kv, head_size).astype(jnp.float32)
    pooled_keys = jnp.concatenate(
        [key_blocks.max(1), key_blocks.min(1), key_blocks.mean(1)], axis=-1
    ).astype(jnp.bfloat16)
    key_proj = jnp.einsum(
        "cgd,gde->cge", pooled_keys, gate_key_weight, preferred_element_type=jnp.float32
    )
    all_key_proj = lax.all_gather(key_proj, "ctx", axis=0, tiled=True)
    first_half = queries[:half_rows]
    second_half = queries[half_rows:]
    first_start = ctx_rank * local_rows
    second_start = first_start + half_rows
    first_group = first_half.reshape(half_rows, local_kv, repeats, head_size)
    second_group = second_half.reshape(half_rows, local_kv, repeats, head_size)
    row_offsets = jnp.arange(half_rows, dtype=jnp.int32)
    first_positions = first_start + row_offsets
    second_positions = second_start + row_offsets
    first_lowest = doc_start[first_positions // BLK] * BLK
    second_lowest = doc_start[second_positions // BLK] * BLK
    initial = (
        jnp.full((local_heads, half_rows), -1e30, jnp.float32),
        jnp.zeros((local_heads, half_rows), jnp.float32),
        jnp.full((local_heads, half_rows, block_count), -1e30, jnp.float32),
    )
    key_piece = lax.all_gather(keys, "ctx", axis=0, tiled=True)
    piece_start = jnp.int32(0)
    first_state = absorb(
        initial, first_group, first_positions, first_lowest, key_piece, piece_start, score_scale
    )
    second_state = absorb(
        initial, second_group, second_positions, second_lowest, key_piece, piece_start, score_scale
    )
    first_state, second_state = (first_state, second_state)
    first_targets, first_pooled, first_qgrad, first_kgrad = finish(
        first_state,
        first_group,
        first_start,
        doc_start,
        all_key_proj,
        gate_query_weight,
        gate_scale,
    )
    second_targets, second_pooled, second_qgrad, second_kgrad = finish(
        second_state,
        second_group,
        second_start,
        doc_start,
        all_key_proj,
        gate_query_weight,
        gate_scale,
    )
    block_targets = jnp.concatenate([first_targets, second_targets], axis=1)
    key_proj_grad = lax.psum_scatter(
        first_kgrad + second_kgrad, "ctx", scatter_dimension=0, tiled=True
    )
    pooled_queries = jnp.concatenate([first_pooled, second_pooled], axis=0)
    query_grads = jnp.concatenate([first_qgrad, second_qgrad], axis=0)
    query_weight_part = jnp.einsum(
        "ahd,ahe->hde",
        pooled_queries.astype(jnp.float32),
        query_grads,
        precision=lax.Precision.HIGHEST,
    )
    key_weight_part = jnp.einsum(
        "cgd,cge->gde",
        pooled_keys.astype(jnp.float32),
        key_proj_grad,
        precision=lax.Precision.HIGHEST,
    )
    query_weight_grad, key_weight_grad = lax.psum((query_weight_part, key_weight_part), "ctx")
    return (block_targets, key_proj_grad, query_weight_grad, key_weight_grad)


def solution(mesh):
    placed = (
        P(("groups", "ctx"), "head", None),
        P(("groups", "ctx"), "head", None),
        P("groups"),
        P("head", None, None),
        P("head", None, None),
    )
    return jax.shard_map(
        per_device,
        mesh=mesh,
        in_specs=placed,
        out_specs=(
            P("head", ("groups", "ctx"), None),
            P(("groups", "ctx"), "head", None),
            P(("groups", "head"), None, None),
            P(("groups", "head"), None, None),
        ),
        check_vma=False,
    )
```

profile of v0, /device:TPU:0, one launch (start us, length us, event | category | flops | bytes accessed | tf_op | source)
XLA Modules:
  0.0 288.9 jit_solution(4135075685758070492)
XLA Ops:
  7.3 1.7 copy.122
  9.1 1.0 convert_reduce_fusion.2
  10.1 1.1 bitcast_reduce_fusion.1
  11.2 0.8 reduce-window.9
  12.8 1.2 gather_fusion.3
  14.6 1.3 slice.21
  18.6 1.2 gather_fusion.1
  22.4 32.2 %all_gather.7 = f32[32,2,128]{2,1,0:T(2,128)S(1)} all-gather(f32[4,2,128]{2,1,0:T(2,128)S(1)} %copy.133), channel_id=1, replica_groups=mesh['groups'=2,'ctx'=8,'head'=2] {'ctx'}, dimensions={0}, use_global_device_ids=true | all-gather | bytes 36864 | tf_op jit(solution)/shard_map/all_gather | solution.py:123
  58.1 1.3 fusion.50
  60.2 44.2 %conditional.2 = (f32[10,128]{1,0:T(8,128)}, f32[10,128,32]{1,2,0:T(8,128)}, f32[10,128]{1,0:T(8,128)S(1)}) conditional(s32[]{:T(128)} %bitcast.6, () %tuple.52, (bf16[128,10,128]{2,0,1:T(8,128)(2,1)}, s32[4]{0:T(128)S(1)}, s32[128]{0:T(128)S(1)}, s32[128]{0:T(128)S(1)}, bf16[4,512,2,128]{3,1,0,2:T(8,128)(2,1)}) %tuple.128), branch_computations={%region_2.3_spmd, %region_3.9_spmd} | conditional | flops 174061824 | bytes 9186832 | solution.py:49
  60.9 43.6 %while.32 = (s32[]{:T(128)}, f32[10,128]{1,0:T(8,128)}, f32[10,128]{1,0:T(8,128)S(1)}, f32[10,128,32]{1,2,0:T(8,128)}, s32[4]{0:T(128)S(1)}, /*index=5*/s32[128]...) while((s32[]{:T(128)}, f32[10,128]{1,0:T(8,128)}, ...), condition=%wide.region_8.8_spmd.clone, body=%wide.region_4.7_spmd.clone.sunk | while | flops 174061824 | bytes 9012596 | solution.py:43
  62.4 1.6 fusion.73
  69.3 1.5 dynamic_update_slice.17
  72.2 1.6 fusion.73
  80.5 1.5 dynamic_update_slice.17
  83.5 1.6 fusion.73
  91.8 1.5 dynamic_update_slice.17
  94.7 1.6 fusion.73
  103.0 1.4 dynamic_update_slice.17
  105.1 0.9 subtract_exponential_fusion.1
  107.1 1.0 convolution_bitcast_fusion.1
  108.1 0.8 fusion.20
  108.9 47.0 %conditional.3 = (f32[10,128]{1,0:T(8,128)}, f32[10,128,32]{1,2,0:T(8,128)}, f32[10,128]{1,0:T(8,128)}) conditional(s32[]{:T(128)} %bitcast.10, () %tuple.54, (bf16[128,10,128]{2,0,1:T(8,128)(2,1)S(1)}, s32[4]{0:T(128)S(1)}, s32[128]{0:T(128)}, s32[128]{0:T(128)}, bf16[4,512,2,128]{3,1,0,2:T(8,128)(2,1)}) %tuple.129), branch_computations={%region_11.12_spmd, %region_12.18_spmd} | conditional | flops 174061824 | bytes 9187016 | solution.py:49
  109.6 45.8 %while.33 = (s32[]{:T(128)}, f32[10,128]{1,0:T(8,128)}, f32[10,128]{1,0:T(8,128)S(1)}, f32[10,128,32]{1,2,0:T(8,128)}, s32[4]{0:T(128)S(1)}, /*index=5*/s32[128]...) while((s32[]{:T(128)}, f32[10,128]{1,0:T(8,128)}, ...), condition=%wide.region_17.17_spmd.clone, body=%wide.region_13.16_spmd.clone.sunk | while | flops 174061824 | bytes 9012780 | solution.py:43
  110.8 0.8 compare_and_fusion.10
  111.6 1.5 fusion.70
  114.9 0.8 compare_and_fusion.11
  118.6 1.5 dynamic_update_slice.16
  121.2 0.8 compare_and_fusion.10
  122.0 1.5 fusion.70
  126.7 0.8 compare_and_fusion.11
  130.3 1.5 dynamic_update_slice.16
  133.0 0.8 compare_and_fusion.10
  133.8 1.5 fusion.70
  142.1 1.5 dynamic_update_slice.16
  144.8 0.8 compare_and_fusion.10
  145.6 1.5 fusion.70
  150.3 0.8 compare_and_fusion.11
  153.9 1.4 dynamic_update_slice.16
  156.7 0.9 subtract_exponential_fusion
  159.4 1.0 fusion.19
  160.4 1.1 fusion.14
  161.6 37.1 %all-reduce = f32[32,2,128]{2,0,1:T(8,128)S(1)} all-reduce(f32[32,2,128]{2,0,1:T(8,128)S(1)} %fusion.14), channel_id=2, replica_groups=mesh['groups'=2,'ctx'=8,'head'=2] {'ctx'}, use_global_device_ids=true, to_apply=%region_29.30.clone | all-reduce | flops 8192 | bytes 65536
  199.4 1.8 fusion.47
  201.2 1.3 fusion.29
  204.1 74.2 %all-reduce.4.cloned.1.call-done = (f32[10,128,128]{2,1,0:T(8,128)}, f32[2,384,128]{2,1,0:T(8,128)}) async-done(((f32[10,128,128]{2,1,0:T(8,128)}, f32[2,384,128]{2,1,0:T(8,128)}), (f32[10,128,128]{2,1,0:T(8,128)}, f32[2,384,128]{2,1,0:T(8,128)})) %all-reduce.4.cloned.1.call-update) | async-done | bytes 1048592 | tf_op jit(solution)/shard_map/psum | solution.py:185
  278.4 2.0 copy.238
  280.3 1.8 copy.239
  (225 shorter events, 55.3 us)
Async XLA Ops:
  7.2 48.7 %copy-start = (bf16[10,128,128]{2,1,0:T(8,128)(2,1)S(1)}, bf16[10,128,128]{2,1,0:T(8,128)(2,1)}, u32[]{:S(2)}) copy-start(bf16[10,128,128]{2,1,0:T(8,128)(2,1)} %param.16) | copy-start | bytes 983044
  7.2 47.4 %copy-start.20 = (u32[32]{0:T(128)S(1)}, u32[32]{0:T(128)}, u32[]{:S(2)}) copy-start(u32[32]{0:T(128)} %constant.253) | copy-start | bytes 388
  7.2 14.8 %copy-start.1 = (bf16[256,10,128]{2,0,1:T(8,128)(2,1)S(1)}, bf16[256,10,128]{2,0,1:T(8,128)(2,1)}, u32[]{:S(2)}) copy-start(bf16[256,10,128]{2,0,1:T(8,128)(2,1)} %param.13) | copy-start | bytes 1966084
  7.2 15.0 %copy-start.3 = (bf16[2,384,128]{2,1,0:T(8,128)(2,1)S(1)}, bf16[2,384,128]{2,1,0:T(8,128)(2,1)}, u32[]{:S(2)}) copy-start(bf16[2,384,128]{2,1,0:T(8,128)(2,1)} %param.17) | copy-start | bytes 589828
  7.2 53.0 %all-gather.2.cloned.1.call-start = ((), (), s32[]{:S(2)}) async-start(), calls=%async_computation | async-start | bytes 1179648 | tf_op jit(solution)/shard_map/all_gather | solution.py:140
  8.9 269.4 %all-reduce.4.cloned.1.call-start = ((), (), s32[]{:S(2)}) async-start(), calls=%async_computation.1 | async-start | bytes 2097152 | tf_op jit(solution)/shard_map/psum | solution.py:185
  17.9 39.8 %copy-start.17 = (pred[2,32]{1,0:T(4,128)(4,1)}, pred[2,32]{1,0:T(4,128)(4,1)S(1)}, u32[]{:S(2)}) copy-start(pred[2,32]{1,0:T(4,128)(4,1)S(1)} %compare_and_fusion.4) | copy-start | bytes 196
  22.0 84.7 %copy-start.12 = (pred[2,32]{0,1:T(8,128)(4,1)}, pred[2,32]{0,1:T(8,128)(4,1)S(1)}, u32[]{:S(2)}) copy-start(pred[2,32]{0,1:T(8,128)(4,1)S(1)} %copy.121) | copy-start | bytes 196
  22.2 33.7 %copy-start.14 = (bf16[4,2,128]{2,0,1:T(4,128)(2,1)}, bf16[4,2,128]{2,0,1:T(4,128)(2,1)S(1)}, u32[]{:S(2)}) copy-start(bf16[4,2,128]{2,0,1:T(4,128)(2,1)S(1)} %fusion.40) | copy-start | bytes 6148
  22.2 35.5 %copy-start.15 = (bf16[4,2,128]{2,0,1:T(4,128)(2,1)}, bf16[4,2,128]{2,0,1:T(4,128)(2,1)S(1)}, u32[]{:S(2)}) copy-start(bf16[4,2,128]{2,0,1:T(4,128)(2,1)S(1)} %copy.132) | copy-start | bytes 6148
  22.2 35.5 %copy-start.16 = (bf16[4,2,128]{2,0,1:T(4,128)(2,1)}, bf16[4,2,128]{2,0,1:T(4,128)(2,1)S(1)}, u32[]{:S(2)}) copy-start(bf16[4,2,128]{2,0,1:T(4,128)(2,1)S(1)} %copy.131) | copy-start | bytes 6148
  54.6 53.5 %copy-start.2 = (f32[32,2,128]{2,1,0:T(2,128)}, f32[32,2,128]{2,1,0:T(2,128)S(1)}, u32[]{:S(2)}) copy-start(f32[32,2,128]{2,1,0:T(2,128)S(1)} %all_gather.7) | copy-start | bytes 98308
  55.9 0.6 copy-start.9
  55.9 1.6 copy-start.7
  57.5 0.6 copy-start.6
  106.8 2.1 copy-start.4
  109.6 0.6 copy-start.18
  113.7 6.3 %copy-start.19 = (s32[4]{0:T(128)S(1)}, s32[4]{0:T(128)}, u32[]{:S(2)}) copy-start(s32[4]{0:T(128)} %copy-done.18) | copy-start | bytes 52 | tf_op jit(solution)/shard_map/cond/branch_1_fun/while
  120.0 0.6 copy-start.18
  124.8 7.0 %copy-start.19 = (s32[4]{0:T(128)S(1)}, s32[4]{0:T(128)}, u32[]{:S(2)}) copy-start(s32[4]{0:T(128)} %copy-done.18) | copy-start | bytes 52 | tf_op jit(solution)/shard_map/cond/branch_1_fun/while
  131.8 0.6 copy-start.18
  136.6 7.0 %copy-start.19 = (s32[4]{0:T(128)S(1)}, s32[4]{0:T(128)}, u32[]{:S(2)}) copy-start(s32[4]{0:T(128)} %copy-done.18) | copy-start | bytes 52 | tf_op jit(solution)/shard_map/cond/branch_1_fun/while
  143.6 0.6 copy-start.18
  148.4 7.0 %copy-start.19 = (s32[4]{0:T(128)S(1)}, s32[4]{0:T(128)}, u32[]{:S(2)}) copy-start(s32[4]{0:T(128)} %copy-done.18) | copy-start | bytes 52 | tf_op jit(solution)/shard_map/cond/branch_1_fun/while
  156.0 45.3 %copy-start.8 = (bf16[2,10,128]{2,0,1:T(2,128)(2,1)S(1)}, bf16[2,10,128]{2,0,1:T(2,128)(2,1)}, u32[]{:S(2)}) copy-start(bf16[2,10,128]{2,0,1:T(2,128)(2,1)} %copy-done.7) | copy-start | bytes 15364
  156.0 45.3 %copy-start.10 = (bf16[2,10,128]{2,0,1:T(2,128)(2,1)S(1)}, bf16[2,10,128]{2,0,1:T(2,128)(2,1)}, u32[]{:S(2)}) copy-start(bf16[2,10,128]{2,0,1:T(2,128)(2,1)} %copy-done.9) | copy-start | bytes 15364
  156.0 47.2 %copy-start.11 = (pred[2,32]{0,1:T(8,128)(4,1)S(1)}, pred[2,32]{0,1:T(8,128)(4,1)}, u32[]{:S(2)}) copy-start(pred[2,32]{0,1:T(8,128)(4,1)} %copy.125) | copy-start | bytes 196
  156.0 47.3 %copy-start.5 = (f32[10,2]{1,0:T(8,128)S(1)}, f32[10,2]{1,0:T(8,128)}, u32[]{:S(2)}) copy-start(f32[10,2]{1,0:T(8,128)} %copy-done.4) | copy-start | bytes 244
  156.0 47.3 %copy-start.13 = (pred[2,32]{0,1:T(8,128)(4,1)S(1)}, pred[2,32]{0,1:T(8,128)(4,1)}, u32[]{:S(2)}) copy-start(pred[2,32]{0,1:T(8,128)(4,1)} %copy-done.12) | copy-start | bytes 196
Sparse Core Ops, SparseCore 0:
  10.8 42.9 all-gather.1
  202.7 75.6 all-reduce.3
where the time goes:
time: 291 us; the launch traced here: 289 us
  waiting for transfers between devices  74.3 us (26%)
  blocking collectives  69.4 us (24%)
  other arithmetic  46.8 us (16%)
  local copies, waits for them, and re-layouts  40.1 us (14%)
  loops' own time  20.9 us (7%)
  matrix products  20.3 us (7%)
  between operations  17.1 us (6%)
    psum x1, waiting for transfers between devices, per_device(): lax.psum((query_weight_part, key_weight_part), 'ctx')  74.2 us
    unnamed x1, blocking collectives  37.1 us
    all_gather x1, blocking collectives, per_device(): all_key_proj = lax.all_gather(key_proj, 'ctx', axis=0, tiled=True)  32.2 us
    another operation x2, loops' own time, do_work(): return lax.scan(one_tile, carried, (key_tiles, tile_offsets))[0]  20.9 us
    dot_general x8, matrix products, one_tile(): jnp.einsum('rgfd,ngd->gfrn', query_group, key_tile, preferred_element_typ...  12.4 us
    dynamic_update_slice x8, local copies, waits for them, and re-layouts, one_tile(): lax.dynamic_update_slice(block_best, tile_best, (jnp.int32(0), jnp.int32(...  11.6 us
    add x16, other arithmetic, one_tile(): key_positions = tile_offset + jnp.arange(tile_width, dtype=jnp.int32)  10.1 us
    and x16, other arithmetic, one_tile(): (key_positions[None, :] <= positions[:, None]) & (key_positions[None, :]...  7.65 us
  transfers between devices with their start and end apart: 2, of which 1 were waited for; matrix products, arithmetic and copies ran while one was open for 6% of the time, Pallas kernels for 0%

commit v1 on v0

v1 whole, which is shorter than its diff:
```python
import functools
import math

import jax
import jax.numpy as jnp
from jax import lax
from jax.experimental import pallas as pl
from jax.experimental.pallas import tpu as pltpu
from jax.sharding import PartitionSpec as P

BLK = 64
LOG2E = 1.4426950408889634
LOW = -1e30
VMEM_LIMIT = 60 * 1024 * 1024
F32 = jnp.float32
BF16 = jnp.bfloat16


def dot(a, b, a_dim, b_dim, precision=None):
    return lax.dot_general(
        a, b, (((a_dim,), (b_dim,)), ((), ())), precision=precision, preferred_element_type=F32
    )


def exact_dot(a, b, a_dim, b_dim):
    return dot(a, b, a_dim, b_dim, lax.Precision.HIGHEST)


def doc_begins(lengths_ref):
    begins, total = [], jnp.int32(0)
    for doc in range(lengths_ref.shape[0]):
        begins.append(total)
        total = total + lengths_ref[doc]
    return begins


def start_of(begins, block):
    start = jnp.zeros_like(block)
    for begin in begins:
        start = jnp.maximum(start, jnp.where(begin <= block, begin, 0))
    return start


def prep_kernel(q_ref, k_ref, packed_ref):
    rows, width = k_ref.shape
    heads, _, head_size = q_ref.shape
    blocks = rows // BLK
    per_row = width // head_size
    packed_ref[0:rows, :] = k_ref[...]
    pooled = []
    for head in range(heads):
        values = q_ref[head].astype(F32).reshape(blocks, BLK, head_size)
        pooled.append(jnp.sum(values, axis=1) * (1.0 / BLK))
    lines = [
        jnp.concatenate(pooled[at : at + per_row], axis=1) for at in range(0, heads, per_row)
    ]
    spare = packed_ref.shape[0] - rows - blocks * len(lines)
    lines.append(jnp.zeros((spare, width), F32))
    packed_ref[rows:, :] = jnp.concatenate(lines, axis=0).astype(BF16)


def attention_kernel(scale, ranks, lengths_ref, q_ref, *refs):
    pieces = refs[:ranks]
    targets_ref, sent_ref, pooled_q_ref, pooled_k_ref = refs[ranks : ranks + 4]
    best_ref, sum_ref, pk_ref, pq_ref = refs[ranks + 4 :]
    heads, rows, head_size = q_ref.shape
    width = pieces[0].shape[1]
    kv = width // head_size
    repeats = heads // kv
    blocks = rows // BLK
    block_count = blocks * ranks
    me = lax.axis_index("ctx")
    begins = doc_begins(lengths_ref)
    first_needed = start_of(begins, me * blocks)
    causal = lax.broadcasted_iota(jnp.int32, (rows, rows), 0) <= lax.broadcasted_iota(
        jnp.int32, (rows, rows), 1
    )

    for step in range(ranks):
        piece = pieces[step]
        source = me ^ step
        keys = piece[0:rows, :].astype(F32).reshape(blocks, BLK, width)
        stats = (jnp.max(keys, 1), jnp.min(keys, 1), jnp.sum(keys, 1) * (1.0 / BLK))
        for group in range(kv):
            for at, value in enumerate(stats):
                pk_ref[group, source, :, at * head_size : (at + 1) * head_size] = value[
                    :, group * head_size : (group + 1) * head_size
                ]
        tail = piece[rows:, :].astype(F32)
        for head in range(heads):
            line, part = head // kv, head % kv
            pq_ref[head, source] = tail[
                line * blocks : (line + 1) * blocks, part * head_size : (part + 1) * head_size
            ]

        @pl.when((source <= me) & (source * blocks + blocks > first_needed))
        def _(step=step, piece=piece, source=source):
            for group in range(kv):
                key_rows = piece[0:rows, group * head_size : (group + 1) * head_size]
                for head in range(group * repeats, (group + 1) * repeats):
                    scores = dot(key_rows, q_ref[head], 1, 1)
                    if step == 0:
                        scores = jnp.where(causal, scores, LOW)
                    scores = scores.reshape(blocks, BLK, rows)
                    best = jnp.max(scores, axis=1)
                    total = jnp.sum(jnp.exp2((scores - best[:, None, :]) * scale), axis=1)
                    best_ref[head, source] = best
                    sum_ref[head, source] = total

    shape = (ranks, blocks, rows)
    key_block = lax.broadcasted_iota(jnp.int32, shape, 0) * blocks + lax.broadcasted_iota(
        jnp.int32, shape, 1
    )
    query_block = me * blocks + lax.broadcasted_iota(jnp.int32, shape, 2) // BLK
    valid = (key_block <= query_block) & (key_block >= start_of(begins, query_block))
    lane = lax.broadcasted_iota(jnp.int32, (ranks, blocks, 128), 2)
    gathered = jnp.zeros((ranks, blocks, 128), F32)
    for head in range(heads):
        best = jnp.where(valid, best_ref[head], LOW)
        top = jnp.max(jnp.max(best, axis=0, keepdims=True), axis=1, keepdims=True)
        shifted = (best - top) * scale
        total = jnp.where(valid, sum_ref[head] * jnp.exp2(shifted), 0.0)
        total = jnp.sum(jnp.sum(total, axis=0, keepdims=True), axis=1, keepdims=True)
        ratio = jnp.where(valid, shifted - jnp.log2(total), LOW)
        for block in range(blocks):
            part = ratio[:, :, block * BLK // 128 * 128 : (block * BLK // 128 + 1) * 128]
            inside = (lane // BLK) == (block % (128 // BLK))
            high = jnp.max(jnp.where(inside, part, LOW), axis=2, keepdims=True)
            gathered = jnp.where(lane == head * blocks + block, high, gathered)
    raw = jnp.exp2(gathered)
    norm = jnp.sum(jnp.sum(raw, axis=0, keepdims=True), axis=1, keepdims=True)
    final = (raw / norm).reshape(block_count, 128)
    if block_count < 128:
        final = jnp.concatenate([final, jnp.zeros((128 - block_count, 128), F32)], axis=0)
    final = final.T
    sent_ref[...] = final[0 : heads * blocks]
    for head in range(heads):
        targets_ref[head] = final[head * blocks : (head + 1) * blocks, 0:block_count]
        pooled_q_ref[head] = pq_ref[head].reshape(block_count, head_size).astype(BF16)
    for group in range(kv):
        pooled_k_ref[group] = pk_ref[group].reshape(block_count, 3 * head_size).astype(BF16)


def gate_kernel(
    scale,
    ranks,
    lengths_ref,
    all_targets_ref,
    pooled_q_ref,
    pooled_k_ref,
    wq_ref,
    wk_ref,
    key_grad_ref,
    wq_grad_ref,
    wk_grad_ref,
    own_ref,
):
    heads, block_count, head_size = pooled_q_ref.shape
    kv = pooled_k_ref.shape[0]
    repeats = heads // kv
    blocks = block_count // ranks
    me = lax.axis_index("ctx")
    begins = doc_begins(lengths_ref)
    shape = (repeats * block_count, block_count)
    query_block = lax.broadcasted_iota(jnp.int32, shape, 0) % block_count
    key_block = lax.broadcasted_iota(jnp.int32, shape, 1)
    valid = (key_block <= query_block) & (key_block >= start_of(begins, query_block))
    for group in range(kv):
        members = range(group * repeats, (group + 1) * repeats)
        pooled_k = pooled_k_ref[group]
        key_proj = dot(pooled_k, wk_ref[group], 1, 0)
        query_proj = jnp.concatenate(
            [dot(pooled_q_ref[head], wq_ref[head], 1, 0) for head in members], axis=0
        )
        logits = jnp.where(valid, exact_dot(query_proj, key_proj, 1, 1) * scale, LOW)
        weights = jnp.exp(logits - jnp.max(logits, axis=1, keepdims=True))
        probs = weights / jnp.sum(weights, axis=1, keepdims=True)
        targets = jnp.concatenate(
            [
                all_targets_ref[:, head * blocks : (head + 1) * blocks, :].reshape(block_count, 128)[
                    :, 0:block_count
                ]
                for head in members
            ],
            axis=0,
        )
        delta = jnp.where(valid, probs - targets, 0.0)
        query_grad = exact_dot(delta, key_proj, 1, 0) * scale
        key_grad = exact_dot(delta, query_proj, 0, 0) * scale
        for at, head in enumerate(members):
            wq_grad_ref[head] = exact_dot(
                pooled_q_ref[head].astype(F32),
                query_grad[at * block_count : (at + 1) * block_count],
                0,
                0,
            )
        wk_grad_ref[group] = exact_dot(pooled_k.astype(F32), key_grad, 0, 0)
        own_ref[...] = key_grad.reshape(ranks, blocks, head_size)
        key_grad_ref[:, group, :] = own_ref[me]


def per_device(queries, keys, doc_lengths, gate_query_weight, gate_key_weight):
    rows, heads, head_size = queries.shape
    kv = keys.shape[1]
    ranks = lax.axis_size("ctx")
    blocks = rows // BLK
    block_count = blocks * ranks
    width = kv * head_size
    extra = -(-(blocks * heads // kv) // 16) * 16
    params = pltpu.CompilerParams(vmem_limit_bytes=VMEM_LIMIT)
    smem = pl.BlockSpec(memory_space=pltpu.SMEM)
    vmem = pl.BlockSpec(memory_space=pltpu.VMEM)

    head_queries = queries.transpose(1, 0, 2)
    flat_keys = keys.reshape(rows, width)
    packed = pl.pallas_call(
        prep_kernel,
        out_shape=jax.ShapeDtypeStruct((rows + extra, width), BF16),
        in_specs=[vmem, vmem],
        out_specs=vmem,
        compiler_params=params,
        name="pool_queries",
    )(head_queries, flat_keys)
    pieces = [packed] + [
        lax.ppermute(packed, "ctx", [(i, i ^ step) for i in range(ranks)])
        for step in range(1, ranks)
    ]
    block_targets, sent, pooled_q, pooled_k = pl.pallas_call(
        functools.partial(attention_kernel, LOG2E / math.sqrt(head_size), ranks),
        out_shape=(
            jax.ShapeDtypeStruct((heads, blocks, block_count), F32),
            jax.ShapeDtypeStruct((heads * blocks, 128), F32),
            jax.ShapeDtypeStruct((heads, block_count, head_size), BF16),
            jax.ShapeDtypeStruct((kv, block_count, 3 * head_size), BF16),
        ),
        in_specs=[smem] + [vmem] * (1 + ranks),
        out_specs=(vmem,) * 4,
        scratch_shapes=[
            pltpu.VMEM((heads, ranks, blocks, rows), F32),
            pltpu.VMEM((heads, ranks, blocks, rows), F32),
            pltpu.VMEM((kv, ranks, blocks, 3 * head_size), F32),
            pltpu.VMEM((heads, ranks, blocks, head_size), F32),
        ],
        compiler_params=params,
        name="block_max_attention",
    )(doc_lengths, head_queries, *pieces)
    all_targets = lax.all_to_all(
        jnp.broadcast_to(sent[None], (ranks,) + sent.shape), "ctx", 0, 0
    )
    key_proj_grad, query_weight_grad, key_weight_grad = pl.pallas_call(
        functools.partial(gate_kernel, 1.0 / math.sqrt(gate_query_weight.shape[2]), ranks),
        out_shape=(
            jax.ShapeDtypeStruct((blocks, kv, head_size), F32),
            jax.ShapeDtypeStruct(gate_query_weight.shape, F32),
            jax.ShapeDtypeStruct(gate_key_weight.shape, F32),
        ),
        in_specs=[smem] + [vmem] * 5,
        out_specs=(vmem,) * 3,
        scratch_shapes=[pltpu.VMEM((ranks, blocks, head_size), F32)],
        compiler_params=params,
        name="gate_gradients",
    )(doc_lengths, all_targets, pooled_q, pooled_k, gate_query_weight, gate_key_weight)
    return (block_targets, key_proj_grad, query_weight_grad, key_weight_grad)


def solution(mesh):
    placed = (
        P(("groups", "ctx"), "head", None),
        P(("groups", "ctx"), "head", None),
        P("groups"),
        P("head", None, None),
        P("head", None, None),
    )
    return jax.shard_map(
        per_device,
        mesh=mesh,
        in_specs=placed,
        out_specs=(
            P("head", ("groups", "ctx"), None),
            P(("groups", "ctx"), "head", None),
            P(("groups", "head"), None, None),
            P(("groups", "head"), None, None),
        ),
        check_vma=False,
    )
```

time: 291 us -> 63.3 us (0.22)
  waiting for transfers between devices: 74.3 us -> 7.54 us
  blocking collectives: 69.4 us -> 15.7 us
  other arithmetic: 46.8 us -> 0 us
  local copies, waits for them, and re-layouts: 40.1 us -> 3.6 us
  starting transfers between devices: 0.08 us -> 25.2 us
  loops' own time: 20.9 us -> 0 us
  matrix products: 20.3 us -> 0 us
  between operations: 17.1 us -> 0.68 us
  Pallas kernels: 0 us -> 10.6 us
    psum x1 -> x0, waiting for transfers between devices: 74.2 us -> none  [per_device(): lax.psum((query_weight_part, key_weight_part), 'ctx')]
    unnamed x1 -> x0, blocking collectives: 37.1 us -> none
    all_gather x1 -> x0, blocking collectives: 32.2 us -> none  [per_device(): all_key_proj = lax.all_gather(key_proj, 'ctx', axis=0, tiled=True)]
    ppermute x0 -> x7, starting transfers between devices: none -> 25.2 us  [per_device(): lax.ppermute(packed, 'ctx', [(i, i ^ step) for i in range(ranks)])]
    another operation x4 -> x0, loops' own time: 20.9 us -> none  [the longest x2 20.9 us: do_work(): return lax.scan(one_tile, carried, (key_tiles, tile_offsets))[0]]
    dot_general x19 -> x0, matrix products: 20.3 us -> none  [the longest x8 12.4 us: one_tile(): jnp.einsum('rgfd,ngd->gfrn', query_group, key_tile, preferred_element_typ...]
    add x30 -> x0, other arithmetic: 16.5 us -> none  [the longest x16 10.1 us: one_tile(): key_positions = tile_offset + jnp.arange(tile_width, dtype=jnp.int32)]
    all_to_all x0 -> x1, blocking collectives: none -> 15.7 us  [per_device(): lax.all_to_all(jnp.broadcast_to(sent[None], (ranks,) + sent.shape), 'ctx'...]
  transfers between devices with their start and end apart: 2 -> 7, of which waited for: 1 -> 3; matrix products, arithmetic and copies ran while one was open for 6% -> 0% of each run, Pallas kernels for 0% -> 0%
where the time goes in v1:
time: 63.3 us; the launch traced here: 63.4 us
  starting transfers between devices  25.2 us (40%)
  blocking collectives  15.7 us (25%)
  Pallas kernels  10.6 us (17%)
  waiting for transfers between devices  7.54 us (12%)
  local copies, waits for them, and re-layouts  3.6 us (6%)
  between operations  0.68 us (1%)
    ppermute x7, starting transfers between devices, per_device(): lax.ppermute(packed, 'ctx', [(i, i ^ step) for i in range(ranks)])  25.2 us
    all_to_all x1, blocking collectives, per_device(): lax.all_to_all(jnp.broadcast_to(sent[None], (ranks,) + sent.shape), 'ctx'...  15.7 us
    ppermute x7, waiting for transfers between devices, per_device(): lax.ppermute(packed, 'ctx', [(i, i ^ step) for i in range(ranks)])  7.54 us
    pallas_call x1, Pallas kernels, per_device(): pl.pallas_call(functools.partial(gate_kernel, 1.0 / math.sqrt(gate_query_...  4.57 us
    pallas_call x1, Pallas kernels, per_device(): pl.pallas_call(functools.partial(attention_kernel, LOG2E / math.sqrt(head...  4.17 us
    unnamed x15, local copies, waits for them, and re-layouts  2.87 us
    pallas_call x1, Pallas kernels, per_device(): pl.pallas_call(prep_kernel, out_shape=jax.ShapeDtypeStruct((rows + extra,...  1.9 us
  transfers between devices with their start and end apart: 7, of which 3 were waited for; matrix products, arithmetic and copies ran while one was open for 0% of the time, Pallas kernels for 0%

profile of v1, /device:TPU:0, one launch (start us, length us, event | category | flops | bytes accessed | tf_op | source)
XLA Modules:
  0.0 63.4 jit_solution(11324591514724426014)
XLA Ops:
  0.6 1.6 %copy.11 = bf16[32,8,2,128]{3,1,2,0:T(8,128)(2,1)} copy(bf16[32,8,2,128]{3,2,1,0:T(2,128)(2,1)} %bitcast.8) | data formatting | bytes 262144
  2.2 1.9 %pool_queries.1.refs_0_ = bf16[288,256]{1,0:T(8,128)(2,1)} custom-call(bf16[10,256,128]{2,1,0:T(8,128)(2,1)} %bitcast.5, bf16[256,256]{1,0:T(8,128)(2,1)} %bitcast.7), custom_call_target="tpu_custom_call" | custom-call | tf_op jit(solution)/shard_map/pool_queries/pallas_call | solution.py:216
  4.1 6.0 %collective-permute-start.6 = (bf16[288,256]{1,0:T(8,128)(2,1)}, bf16[288,256]{1,0:T(8,128)(2,1)S(1)}, u32[]{:S(2)}, u32[]{:S(2)}) collective-permute-start(bf16[288,256]{1,0:T(8,128)(2,1)} %pool_queries.1.refs_0_), channel_id=1, source_target_pairs={{0,14},{2,12},{4,10},{6,8},{8,6},{10,4},{12,2},{14,0},{1,15},{3,13... | collective-permute-start | bytes 442376 | tf_op jit(solution)/shard_map/ppermute | solution.py:225
  10.1 0.2 collective-permute-start.5
  10.3 0.7 %collective-permute-start.4 = (bf16[288,256]{1,0:T(8,128)(2,1)}, bf16[288,256]{1,0:T(8,128)(2,1)S(1)}, u32[]{:S(2)}, u32[]{:S(2)}) collective-permute-start(bf16[288,256]{1,0:T(8,128)(2,1)} %pool_queries.1.refs_0_), channel_id=1, source_target_pairs={{0,10},{2,8},{4,14},{6,12},{8,2},{10,0},{12,6},{14,4},{1,11},{3,9}... | collective-permute-start | bytes 442376 | tf_op jit(solution)/shard_map/ppermute | solution.py:225
  11.1 2.0 %collective-permute-start.3 = (bf16[288,256]{1,0:T(8,128)(2,1)}, bf16[288,256]{1,0:T(8,128)(2,1)S(1)}, u32[]{:S(2)}, u32[]{:S(2)}) collective-permute-start(bf16[288,256]{1,0:T(8,128)(2,1)} %pool_queries.1.refs_0_), channel_id=1, source_target_pairs={{0,8},{2,10},{4,12},{6,14},{8,0},{10,2},{12,4},{14,6},{1,9},{3,11}... | collective-permute-start | bytes 442376 | tf_op jit(solution)/shard_map/ppermute | solution.py:225
  13.0 2.4 %collective-permute-start.2 = (bf16[288,256]{1,0:T(8,128)(2,1)}, bf16[288,256]{1,0:T(8,128)(2,1)S(1)}, u32[]{:S(2)}, u32[]{:S(2)}) collective-permute-start(bf16[288,256]{1,0:T(8,128)(2,1)} %pool_queries.1.refs_0_), channel_id=1, source_target_pairs={{0,6},{2,4},{4,2},{6,0},{8,14},{10,12},{12,10},{14,8},{1,7},{3,5},... | collective-permute-start | bytes 442376 | tf_op jit(solution)/shard_map/ppermute | solution.py:225
  15.4 0.0 collective-permute-done.6.refs_7_
  15.4 0.0 copy-start
  15.4 12.6 %collective-permute-start.1 = (bf16[288,256]{1,0:T(8,128)(2,1)}, bf16[288,256]{1,0:T(8,128)(2,1)S(1)}, u32[]{:S(2)}, u32[]{:S(2)}) collective-permute-start(bf16[288,256]{1,0:T(8,128)(2,1)} %pool_queries.1.refs_0_), channel_id=1, source_target_pairs={{0,4},{2,6},{4,0},{6,2},{8,12},{10,14},{12,8},{14,10},{1,5},{3,7},... | collective-permute-start | bytes 442376 | tf_op jit(solution)/shard_map/ppermute | solution.py:225
  28.0 0.0 collective-permute-done.5.refs_6_
  28.0 0.0 copy-start.1
  28.0 1.3 %collective-permute-start = (bf16[288,256]{1,0:T(8,128)(2,1)}, bf16[288,256]{1,0:T(8,128)(2,1)S(1)}, u32[]{:S(2)}, u32[]{:S(2)}) collective-permute-start(bf16[288,256]{1,0:T(8,128)(2,1)} %pool_queries.1.refs_0_), channel_id=1, source_target_pairs={{0,2},{2,0},{4,6},{6,4},{8,10},{10,8},{12,14},{14,12},{1,3},{3,1},... | collective-permute-start | bytes 442376 | tf_op jit(solution)/shard_map/ppermute | solution.py:225
  29.3 4.0 %collective-permute-done.4.refs_5_ = bf16[288,256]{1,0:T(8,128)(2,1)S(1)} collective-permute-done((bf16[288,256]{1,0:T(8,128)(2,1)}, bf16[288,256]{1,0:T(8,128)(2,1)S(1)}, u32[]{:S(2)}, u32[]{:S(2)}) %collective-permute-start.4) | collective-permute-done | bytes 147488 | tf_op jit(solution)/shard_map/ppermute | solution.py:225
  33.3 0.0 copy-start.2
  33.3 2.2 %collective-permute-done.3.refs_4_ = bf16[288,256]{1,0:T(8,128)(2,1)S(1)} collective-permute-done((bf16[288,256]{1,0:T(8,128)(2,1)}, bf16[288,256]{1,0:T(8,128)(2,1)S(1)}, u32[]{:S(2)}, u32[]{:S(2)}) %collective-permute-start.3) | collective-permute-done | bytes 147488 | tf_op jit(solution)/shard_map/ppermute | solution.py:225
  35.5 0.0 copy-start.3
  35.5 0.0 collective-permute-done.2.refs_3_
  35.6 0.0 copy-start.4
  35.6 1.3 %collective-permute-done.1.refs_2_ = bf16[288,256]{1,0:T(8,128)(2,1)S(1)} collective-permute-done((bf16[288,256]{1,0:T(8,128)(2,1)}, bf16[288,256]{1,0:T(8,128)(2,1)S(1)}, u32[]{:S(2)}, u32[]{:S(2)}) %collective-permute-start.1) | collective-permute-done | bytes 147488 | tf_op jit(solution)/shard_map/ppermute | solution.py:225
  36.9 0.0 copy-start.5
  36.9 0.0 collective-permute-done.refs_1_
  36.9 0.0 copy-done
  36.9 0.0 copy-done.1
  36.9 0.0 copy-done.2
  36.9 0.0 copy-done.3
  36.9 0.0 copy-done.4
  36.9 0.6 copy-done.5
  37.5 0.0 copy-start.6
  37.5 0.7 %copy-done.6 = bf16[288,256]{1,0:T(8,128)(2,1)} copy-done((bf16[288,256]{1,0:T(8,128)(2,1)}, bf16[288,256]{1,0:T(8,128)(2,1)S(1)}, u32[]{:S(2)}) %copy-start.6) | copy-done | bytes 147480
  38.2 4.2 %block_max_attention.1 = (f32[10,4,32]{2,1,0:T(4,128)}, f32[40,128]{1,0:T(8,128)}, bf16[10,32,128]{2,1,0:T(8,128)(2,1)}, bf16[2,32,384]{2,1,0:T(8,128)(2,1)}) custom-call(s32[4]{0:T(128)} %lengths_ref.3, bf16[10,256,128]{2,1,0:T(8,128)(2,1)} %bitcast.6, bf16[288,256]{1,0:T(8,128)(2,1)} %pool_queries.1.refs_0_, bf16[288,256]{1,0:T(8,128)(2,1)} %copy-done.6, ...), custom_call_target="tpu_custom_call" | custom-call | tf_op jit(solution)/shard_map/block_max_attention/pallas_call | solution.py:228
  42.4 0.7 %broadcast_in_dim.2 = f32[8,40,128]{2,1,0:T(8,128)S(1)} broadcast(f32[40,128]{1,0:T(8,128)} %get-tuple-element.12), dimensions={1,2} | broadcast | bytes 184320 | tf_op jit(solution)/shard_map/broadcast_in_dim | solution.py:248
  43.1 15.7 %all_to_all.5.all_targets_ref = f32[8,40,128]{2,1,0:T(8,128)} all-to-all(f32[8,40,128]{2,1,0:T(8,128)S(1)} %broadcast_in_dim.2), channel_id=1, replica_groups=mesh['groups'=2,'ctx'=8,'head'=2] {'ctx'}, dimensions={0} | all-to-all | bytes 327680 | tf_op jit(solution)/shard_map/all_to_all | solution.py:247
  58.8 4.6 %gate_gradients.1 = (f32[4,2,128]{2,1,0:T(2,128)}, f32[10,128,128]{2,1,0:T(8,128)}, f32[2,384,128]{2,1,0:T(8,128)}) custom-call(s32[4]{0:T(128)} %lengths_ref.3, f32[8,40,128]{2,1,0:T(8,128)} %all_to_all.5.all_targets_ref, bf16[10,32,128]{2,1,0:T(8,128)(2,1)} %get-tuple-element.13.pooled_q_ref, bf16[2,32,384]{2,1,0:T(8,128)(2,1)} %get-tuple-element.14.pooled_k_ref, ...), custom_call_target="tpu_custom_call" | custom-call | tf_op jit(solution)/shard_map/gate_gradients/pallas_call | solution.py:250
Async XLA Ops:
  4.1 11.3 %collective-permute-start.6 = (bf16[288,256]{1,0:T(8,128)(2,1)}, bf16[288,256]{1,0:T(8,128)(2,1)S(1)}, u32[]{:S(2)}, u32[]{:S(2)}) collective-permute-start(bf16[288,256]{1,0:T(8,128)(2,1)} %pool_queries.1.refs_0_), channel_id=1, source_target_pairs={{0,14},{2,12},{4,10},{6,8},{8,6},{10,4},{12,2},{14,0},{1,15},{3,13... | collective-permute-start | bytes 442376 | tf_op jit(solution)/shard_map/ppermute | solution.py:225
  10.1 17.9 %collective-permute-start.5 = (bf16[288,256]{1,0:T(8,128)(2,1)}, bf16[288,256]{1,0:T(8,128)(2,1)S(1)}, u32[]{:S(2)}, u32[]{:S(2)}) collective-permute-start(bf16[288,256]{1,0:T(8,128)(2,1)} %pool_queries.1.refs_0_), channel_id=1, source_target_pairs={{0,12},{2,14},{4,8},{6,10},{8,4},{10,6},{12,0},{14,2},{1,13},{3,15... | collective-permute-start | bytes 442376 | tf_op jit(solution)/shard_map/ppermute | solution.py:225
  10.3 23.0 %collective-permute-start.4 = (bf16[288,256]{1,0:T(8,128)(2,1)}, bf16[288,256]{1,0:T(8,128)(2,1)S(1)}, u32[]{:S(2)}, u32[]{:S(2)}) collective-permute-start(bf16[288,256]{1,0:T(8,128)(2,1)} %pool_queries.1.refs_0_), channel_id=1, source_target_pairs={{0,10},{2,8},{4,14},{6,12},{8,2},{10,0},{12,6},{14,4},{1,11},{3,9}... | collective-permute-start | bytes 442376 | tf_op jit(solution)/shard_map/ppermute | solution.py:225
  11.1 24.5 %collective-permute-start.3 = (bf16[288,256]{1,0:T(8,128)(2,1)}, bf16[288,256]{1,0:T(8,128)(2,1)S(1)}, u32[]{:S(2)}, u32[]{:S(2)}) collective-permute-start(bf16[288,256]{1,0:T(8,128)(2,1)} %pool_queries.1.refs_0_), channel_id=1, source_target_pairs={{0,8},{2,10},{4,12},{6,14},{8,0},{10,2},{12,4},{14,6},{1,9},{3,11}... | collective-permute-start | bytes 442376 | tf_op jit(solution)/shard_map/ppermute | solution.py:225
  13.0 22.5 %collective-permute-start.2 = (bf16[288,256]{1,0:T(8,128)(2,1)}, bf16[288,256]{1,0:T(8,128)(2,1)S(1)}, u32[]{:S(2)}, u32[]{:S(2)}) collective-permute-start(bf16[288,256]{1,0:T(8,128)(2,1)} %pool_queries.1.refs_0_), channel_id=1, source_target_pairs={{0,6},{2,4},{4,2},{6,0},{8,14},{10,12},{12,10},{14,8},{1,7},{3,5},... | collective-permute-start | bytes 442376 | tf_op jit(solution)/shard_map/ppermute | solution.py:225
  15.4 21.5 %copy-start = (bf16[288,256]{1,0:T(8,128)(2,1)}, bf16[288,256]{1,0:T(8,128)(2,1)S(1)}, u32[]{:S(2)}) copy-start(bf16[288,256]{1,0:T(8,128)(2,1)S(1)} %collective-permute-done.6.refs_7_) | copy-start | bytes 442372
  15.4 21.5 %collective-permute-start.1 = (bf16[288,256]{1,0:T(8,128)(2,1)}, bf16[288,256]{1,0:T(8,128)(2,1)S(1)}, u32[]{:S(2)}, u32[]{:S(2)}) collective-permute-start(bf16[288,256]{1,0:T(8,128)(2,1)} %pool_queries.1.refs_0_), channel_id=1, source_target_pairs={{0,4},{2,6},{4,0},{6,2},{8,12},{10,14},{12,8},{14,10},{1,5},{3,7},... | collective-permute-start | bytes 442376 | tf_op jit(solution)/shard_map/ppermute | solution.py:225
  28.0 8.9 %copy-start.1 = (bf16[288,256]{1,0:T(8,128)(2,1)}, bf16[288,256]{1,0:T(8,128)(2,1)S(1)}, u32[]{:S(2)}) copy-start(bf16[288,256]{1,0:T(8,128)(2,1)S(1)} %collective-permute-done.5.refs_6_) | copy-start | bytes 442372
  28.0 8.9 %collective-permute-start = (bf16[288,256]{1,0:T(8,128)(2,1)}, bf16[288,256]{1,0:T(8,128)(2,1)S(1)}, u32[]{:S(2)}, u32[]{:S(2)}) collective-permute-start(bf16[288,256]{1,0:T(8,128)(2,1)} %pool_queries.1.refs_0_), channel_id=1, source_target_pairs={{0,2},{2,0},{4,6},{6,4},{8,10},{10,8},{12,14},{14,12},{1,3},{3,1},... | collective-permute-start | bytes 442376 | tf_op jit(solution)/shard_map/ppermute | solution.py:225
  33.3 3.6 %copy-start.2 = (bf16[288,256]{1,0:T(8,128)(2,1)}, bf16[288,256]{1,0:T(8,128)(2,1)S(1)}, u32[]{:S(2)}) copy-start(bf16[288,256]{1,0:T(8,128)(2,1)S(1)} %collective-permute-done.4.refs_5_) | copy-start | bytes 442372
  35.5 1.4 %copy-start.3 = (bf16[288,256]{1,0:T(8,128)(2,1)}, bf16[288,256]{1,0:T(8,128)(2,1)S(1)}, u32[]{:S(2)}) copy-start(bf16[288,256]{1,0:T(8,128)(2,1)S(1)} %collective-permute-done.3.refs_4_) | copy-start | bytes 442372
  35.6 1.4 %copy-start.4 = (bf16[288,256]{1,0:T(8,128)(2,1)}, bf16[288,256]{1,0:T(8,128)(2,1)S(1)}, u32[]{:S(2)}) copy-start(bf16[288,256]{1,0:T(8,128)(2,1)S(1)} %collective-permute-done.2.refs_3_) | copy-start | bytes 442372
  36.9 0.7 %copy-start.5 = (bf16[288,256]{1,0:T(8,128)(2,1)}, bf16[288,256]{1,0:T(8,128)(2,1)S(1)}, u32[]{:S(2)}) copy-start(bf16[288,256]{1,0:T(8,128)(2,1)S(1)} %collective-permute-done.1.refs_2_) | copy-start | bytes 442372
  37.5 0.7 %copy-start.6 = (bf16[288,256]{1,0:T(8,128)(2,1)}, bf16[288,256]{1,0:T(8,128)(2,1)S(1)}, u32[]{:S(2)}) copy-start(bf16[288,256]{1,0:T(8,128)(2,1)S(1)} %collective-permute-done.refs_1_) | copy-start | bytes 442372

commit v2 on v1

v2 whole, which is shorter than its diff:
```python
import functools
import math

import jax
import jax.numpy as jnp
from jax import lax
from jax.experimental import pallas as pl
from jax.experimental.pallas import tpu as pltpu
from jax.sharding import PartitionSpec as P

BLK = 64
LANES = 128
LOG2E = 1.4426950408889634
LOW = -1e30
VMEM_LIMIT = 60 * 1024 * 1024
F32 = jnp.float32
BF16 = jnp.bfloat16


def dot(a, b, a_dim, b_dim, precision=None):
    return lax.dot_general(
        a, b, (((a_dim,), (b_dim,)), ((), ())), precision=precision, preferred_element_type=F32
    )


def halves(value):
    high = value.astype(BF16)
    return high, (value - high.astype(F32)).astype(BF16)


def iota(shape, dim):
    return lax.broadcasted_iota(jnp.int32, shape, dim)


def doc_begins(lengths_ref):
    begins, total = [], jnp.int32(0)
    for doc in range(lengths_ref.shape[0]):
        begins.append(total)
        total = total + lengths_ref[doc]
    return begins


def start_of(begins, block):
    start = jnp.zeros_like(block)
    for begin in begins:
        start = jnp.maximum(start, jnp.where(begin <= block, begin, 0))
    return start


def pool_keys(piece_ref, out_ref, at, head_size):
    rows, width = piece_ref.shape
    keys = piece_ref[...].astype(F32).reshape(rows // BLK, BLK, width)
    stats = (jnp.max(keys, 1), jnp.min(keys, 1), jnp.sum(keys, 1) * (1.0 / BLK))
    for group in range(width // head_size):
        for part, value in enumerate(stats):
            out_ref[group, at, :, part * head_size : (part + 1) * head_size] = value[
                :, group * head_size : (group + 1) * head_size
            ]


def absorb(scale, begins, me, step, piece_ref, q_ref, best_ref, sum_ref, at):
    heads, rows, head_size = q_ref.shape
    kv = piece_ref.shape[1] // head_size
    blocks = rows // BLK
    source = me ^ step
    needed = (source <= me) & (source * blocks + blocks > start_of(begins, me * blocks))

    @pl.when(needed)
    def _():
        if step == 0:
            causal = iota((rows, rows), 0) <= iota((rows, rows), 1)
        for head in range(heads):
            group = head // (heads // kv)
            key_rows = piece_ref[:, group * head_size : (group + 1) * head_size]
            scores = dot(key_rows, q_ref[head], 1, 1)
            if step == 0:
                scores = jnp.where(causal, scores, LOW)
            scores = scores.reshape(blocks, BLK, rows)
            best = jnp.max(scores, axis=1)
            best_ref[head, at] = best
            sum_ref[head, at] = jnp.sum(jnp.exp2((scores - best[:, None, :]) * scale), axis=1)


def early_kernel(scale, steps, lengths_ref, q_ref, wq_ref, *refs):
    pieces = refs[: len(steps)]
    best_ref, sum_ref, pk_ref, pq_ref, proj_ref = refs[len(steps) :]
    heads, rows, head_size = q_ref.shape
    blocks = rows // BLK
    me = lax.axis_index("ctx")
    begins = doc_begins(lengths_ref)
    for head in range(heads):
        values = q_ref[head].astype(F32).reshape(blocks, BLK, head_size)
        pooled = (jnp.sum(values, axis=1) * (1.0 / BLK)).astype(BF16)
        pq_ref[head * blocks : (head + 1) * blocks, :] = pooled.astype(F32)
        proj_ref[head * blocks : (head + 1) * blocks, :] = dot(pooled, wq_ref[head], 1, 0)
    for at, (step, piece_ref) in enumerate(zip(steps, pieces)):
        pool_keys(piece_ref, pk_ref, at, head_size)
        absorb(scale, begins, me, step, piece_ref, q_ref, best_ref, sum_ref, at)


def late_kernel(scale, gate_scale, early_steps, late_steps, lengths_ref, q_ref, wk_ref, *refs):
    count = len(late_steps)
    pieces = refs[:count]
    best_ref, sum_ref, pk_ref, pq_ref, proj_ref = refs[count : count + 5]
    targets_ref, sent_ref, pooled_k_ref, key_proj_ref = refs[count + 5 : count + 9]
    late_best_ref, late_sum_ref, late_pk_ref, all_pk_ref, column_ref = refs[count + 9 :]
    heads, rows, head_size = q_ref.shape
    kv = wk_ref.shape[0]
    blocks = rows // BLK
    ranks = len(early_steps) + count
    block_count = blocks * ranks
    own_rows = heads * blocks
    me = lax.axis_index("ctx")
    begins = doc_begins(lengths_ref)
    for at, (step, piece_ref) in enumerate(zip(late_steps, pieces)):
        pool_keys(piece_ref, late_pk_ref, at, head_size)
        absorb(scale, begins, me, step, piece_ref, q_ref, late_best_ref, late_sum_ref, at)

    steps = tuple(early_steps) + tuple(late_steps)
    for group in range(kv):
        for at, step in enumerate(early_steps):
            all_pk_ref[group, me ^ step] = pk_ref[group, at]
        for at, step in enumerate(late_steps):
            all_pk_ref[group, me ^ step] = late_pk_ref[group, at]
    proj = proj_ref[...]
    logits = jnp.zeros((own_rows, block_count), F32)
    row = iota((own_rows, block_count), 0)
    for group in range(kv):
        pooled_k = all_pk_ref[group].reshape(block_count, 3 * head_size).astype(BF16)
        key_proj = dot(pooled_k, wk_ref[group], 1, 0)
        pooled_k_ref[group] = pooled_k
        key_proj_ref[group] = key_proj
        part = dot(proj, key_proj, 1, 1, lax.Precision.HIGHEST)
        logits = jnp.where(row // (own_rows // kv) == group, part, logits)
    query_block = me * blocks + row % blocks
    key_block = iota((own_rows, block_count), 1)
    allowed = (key_block <= query_block) & (key_block >= start_of(begins, query_block))
    logits = jnp.where(allowed, logits * gate_scale, LOW)
    weights = jnp.exp(logits - jnp.max(logits, axis=1, keepdims=True))
    probs = weights / jnp.sum(weights, axis=1, keepdims=True)

    lane_block = me * blocks + iota((blocks, rows), 1) // BLK
    lane_start = start_of(begins, lane_block)
    valid = []
    for step in steps:
        key_block = (me ^ step) * blocks + iota((blocks, rows), 0)
        valid.append((key_block <= lane_block) & (key_block >= lane_start))
    lane = iota((blocks, LANES), 1)
    columns = [jnp.zeros((blocks, LANES), F32) for _ in steps]
    for head in range(heads):
        best = [best_ref[head, at] for at in range(len(early_steps))]
        best += [late_best_ref[head, at] for at in range(count)]
        total = [sum_ref[head, at] for at in range(len(early_steps))]
        total += [late_sum_ref[head, at] for at in range(count)]
        best = [jnp.where(ok, value, LOW) for ok, value in zip(valid, best)]
        top = jnp.max(functools.reduce(jnp.maximum, best), axis=0, keepdims=True)
        shifted = [(value - top) * scale for value in best]
        total = [
            jnp.where(ok, value * jnp.exp2(shift), 0.0)
            for ok, value, shift in zip(valid, total, shifted)
        ]
        lse = jnp.log2(jnp.sum(functools.reduce(jnp.add, total), axis=0, keepdims=True))
        for at in range(ranks):
            ratio = jnp.where(valid[at], shifted[at] - lse, LOW)
            for block in range(blocks):
                tile = block * BLK // LANES
                inside = (lane // BLK) == (block % (LANES // BLK))
                part = jnp.where(inside, ratio[:, tile * LANES : (tile + 1) * LANES], LOW)
                high = jnp.max(part, axis=1, keepdims=True)
                columns[at] = jnp.where(lane == head * blocks + block, high, columns[at])
    raw = [jnp.exp2(value) for value in columns]
    norm = 1.0 / jnp.sum(functools.reduce(jnp.add, raw), axis=0, keepdims=True)
    for at, step in enumerate(steps):
        column_ref[me ^ step] = raw[at] * norm
    final = column_ref[...].reshape(block_count, LANES)
    if block_count < LANES:
        final = jnp.concatenate([final, jnp.zeros((LANES - block_count, LANES), F32)], axis=0)
    targets = final.T[0:own_rows, 0:block_count]
    for head in range(heads):
        targets_ref[head] = targets[head * blocks : (head + 1) * blocks]

    delta = jnp.where(allowed, probs - targets, 0.0)
    high, low = halves(delta)
    pieces_of_row = [high.astype(F32), low.astype(F32)]
    width = sent_ref.shape[2]
    if width > 2 * block_count:
        pieces_of_row.append(jnp.zeros((own_rows, width - 2 * block_count), F32))
    pooled_q = pq_ref[...]
    if width > head_size:
        pooled_q = jnp.concatenate(
            [pooled_q, jnp.zeros((own_rows, width - head_size), F32)], axis=1
        )
    packed = jnp.concatenate([pooled_q, jnp.concatenate(pieces_of_row, axis=1)], axis=0)
    packed = packed.astype(BF16)
    for rank in range(ranks):
        sent_ref[rank] = packed


def gate_kernel(
    scale, packed_ref, pooled_k_ref, key_proj_ref, wq_ref, key_grad_ref, wq_grad_ref, wk_grad_ref,
    own_ref,
):
    ranks, packed_rows, _ = packed_ref.shape
    kv, block_count, _ = pooled_k_ref.shape
    heads, head_size, _ = wq_ref.shape
    repeats = heads // kv
    blocks = block_count // ranks
    me = lax.axis_index("ctx")
    packed = packed_ref[...].astype(F32)
    for group in range(kv):
        key_high, key_low = halves(key_proj_ref[group] * scale)
        both_keys = jnp.concatenate([key_high, key_high], axis=0)
        pooled, deltas, projected = [], [], []
        for head in range(group * repeats, (group + 1) * repeats):
            rows = packed[:, head * blocks : (head + 1) * blocks, 0:head_size]
            pooled.append(rows.reshape(block_count, head_size).astype(BF16))
            at = packed_rows // 2 + head * blocks
            rows = packed[:, at : at + blocks, :].reshape(block_count, -1)
            deltas.append(rows[:, 0 : 2 * block_count].astype(BF16))
            projected.append(dot(pooled[-1], wq_ref[head], 1, 0))
        delta = jnp.concatenate(deltas, axis=0)
        delta_high = delta[:, 0:block_count]
        query_grad = dot(delta, both_keys, 1, 0) + dot(delta_high, key_low, 1, 0)
        grad_high, grad_low = halves(query_grad)
        for at in range(repeats):
            rows = slice(at * block_count, (at + 1) * block_count)
            wq_grad_ref[group * repeats + at] = dot(
                jnp.concatenate([pooled[at], pooled[at]], axis=0),
                jnp.concatenate([grad_high[rows], grad_low[rows]], axis=0),
                0,
                0,
            )
        proj_high, proj_low = halves(jnp.concatenate(projected, axis=0) * scale)
        main = dot(delta, proj_high, 0, 0)
        key_grad = main[0:block_count] + main[block_count:] + dot(delta_high, proj_low, 0, 0)
        grad_high, grad_low = halves(key_grad)
        pooled_k = pooled_k_ref[group]
        wk_grad_ref[group] = dot(
            jnp.concatenate([pooled_k, pooled_k], axis=0),
            jnp.concatenate([grad_high, grad_low], axis=0),
            0,
            0,
        )
        own_ref[...] = key_grad.reshape(ranks, blocks, head_size)
        key_grad_ref[:, group, :] = own_ref[me]


def per_device(queries, keys, doc_lengths, gate_query_weight, gate_key_weight):
    rows, heads, head_size = queries.shape
    kv = keys.shape[1]
    ranks = lax.axis_size("ctx")
    blocks = rows // BLK
    block_count = blocks * ranks
    own_rows = heads * blocks
    scale = LOG2E / math.sqrt(head_size)
    gate_scale = 1.0 / math.sqrt(gate_query_weight.shape[2])
    params = pltpu.CompilerParams(vmem_limit_bytes=VMEM_LIMIT)
    smem = pl.BlockSpec(memory_space=pltpu.SMEM)
    vmem = pl.BlockSpec(memory_space=pltpu.VMEM)

    def exchange(value, step):
        return lax.ppermute(value, "ctx", [(i, i ^ step) for i in range(ranks)])

    flat_keys = keys.reshape(rows, kv * head_size)
    early_steps = [0, 1] + list(range(2, ranks, 2))
    late_steps = list(range(3, ranks, 2))
    pieces = {0: flat_keys}
    for step in early_steps[1:]:
        pieces[step] = exchange(flat_keys, step)
    for step in late_steps:
        pieces[step] = exchange(pieces[step - 1], 1)

    head_queries = queries.transpose(1, 0, 2)
    stats = jax.ShapeDtypeStruct((heads, len(early_steps), blocks, rows), F32)
    late_stats = pltpu.VMEM((heads, max(len(late_steps), 1), blocks, rows), F32)
    early = pl.pallas_call(
        functools.partial(early_kernel, scale, early_steps),
        out_shape=(
            stats,
            stats,
            jax.ShapeDtypeStruct((kv, len(early_steps), blocks, 3 * head_size), F32),
            jax.ShapeDtypeStruct((own_rows, head_size), F32),
            jax.ShapeDtypeStruct((own_rows, head_size), F32),
        ),
        in_specs=[smem] + [vmem] * (2 + len(early_steps)),
        out_specs=(vmem,) * 5,
        compiler_params=params,
        name="early_key_blocks",
    )(doc_lengths, head_queries, gate_query_weight, *[pieces[s] for s in early_steps])
    width = -(-2 * block_count // LANES) * LANES
    block_targets, sent, pooled_k, key_proj = pl.pallas_call(
        functools.partial(late_kernel, scale, gate_scale, early_steps, late_steps),
        out_shape=(
            jax.ShapeDtypeStruct((heads, blocks, block_count), F32),
            jax.ShapeDtypeStruct((ranks, 2 * own_rows, width), BF16),
            jax.ShapeDtypeStruct((kv, block_count, 3 * head_size), BF16),
            jax.ShapeDtypeStruct((kv, block_count, head_size), F32),
        ),
        in_specs=[smem] + [vmem] * (7 + len(late_steps)),
        out_specs=(vmem,) * 4,
        scratch_shapes=[
            late_stats,
            late_stats,
            pltpu.VMEM((kv, max(len(late_steps), 1), blocks, 3 * head_size), F32),
            pltpu.VMEM((kv, ranks, blocks, 3 * head_size), F32),
            pltpu.VMEM((ranks, blocks, LANES), F32),
        ],
        compiler_params=params,
        name="late_key_blocks",
    )(doc_lengths, head_queries, gate_key_weight, *[pieces[s] for s in late_steps], *early)
    packed = lax.all_to_all(sent, "ctx", 0, 0)
    key_proj_grad, query_weight_grad, key_weight_grad = pl.pallas_call(
        functools.partial(gate_kernel, gate_scale),
        out_shape=(
            jax.ShapeDtypeStruct((blocks, kv, head_size), F32),
            jax.ShapeDtypeStruct(gate_query_weight.shape, F32),
            jax.ShapeDtypeStruct(gate_key_weight.shape, F32),
        ),
        in_specs=[vmem] * 4,
        out_specs=(vmem,) * 3,
        scratch_shapes=[pltpu.VMEM((ranks, blocks, head_size), F32)],
        compiler_params=params,
        name="gate_gradients",
    )(packed, pooled_k, key_proj, gate_query_weight)
    return (block_targets, key_proj_grad, query_weight_grad, key_weight_grad)


def solution(mesh):
    placed = (
        P(("groups", "ctx"), "head", None),
        P(("groups", "ctx"), "head", None),
        P("groups"),
        P("head", None, None),
        P("head", None, None),
    )
    return jax.shard_map(
        per_device,
        mesh=mesh,
        in_specs=placed,
        out_specs=(
            P("head", ("groups", "ctx"), None),
            P(("groups", "ctx"), "head", None),
            P(("groups", "head"), None, None),
            P(("groups", "head"), None, None),
        ),
        check_vma=False,
    )
```

time: 63.3 us -> 47.7 us (0.75)
  starting transfers between devices: 25.2 us -> 11.2 us
  local copies, waits for them, and re-layouts: 3.6 us -> 2.2 us
  blocking collectives: 15.7 us -> 16.9 us
  Pallas kernels: 10.6 us -> 9.62 us
    ppermute x7, starting transfers between devices: 25.2 us -> 11.2 us  [exchange(): return lax.ppermute(value, 'ctx', [(i, i ^ step) for i in range(ranks)])]
    all_to_all x1, blocking collectives: 15.7 us -> 16.9 us  [per_device(): packed = lax.all_to_all(sent, 'ctx', 0, 0)]
    pallas_call x3, Pallas kernels: 10.6 us -> 9.62 us  [the longest x1 3.45 us: per_device(): pl.pallas_call(functools.partial(early_kernel, scale, early_steps), out_s...]
    broadcast_in_dim x1 -> x0, local copies, waits for them, and re-layouts: 0.74 us -> none  [per_device(): jnp.broadcast_to(sent[None], (ranks,) + sent.shape)]
    unnamed x15 -> x17, local copies, waits for them, and re-layouts: 2.87 us -> 2.2 us
  transfers between devices with their start and end apart: 7 -> 7, of which waited for: 3 -> 3; matrix products, arithmetic and copies ran while one was open for 0% -> 0% of each run, Pallas kernels for 0% -> 7%
where the time goes in v2:
time: 47.7 us; the launch traced here: 47.8 us
  blocking collectives  16.9 us (35%)
  starting transfers between devices  11.2 us (23%)
  Pallas kernels  9.62 us (20%)
  waiting for transfers between devices  7.19 us (15%)
  local copies, waits for them, and re-layouts  2.2 us (5%)
  between operations  0.69 us (1%)
    all_to_all x1, blocking collectives, per_device(): packed = lax.all_to_all(sent, 'ctx', 0, 0)  16.9 us
    ppermute x7, starting transfers between devices, exchange(): return lax.ppermute(value, 'ctx', [(i, i ^ step) for i in range(ranks)])  11.2 us
    ppermute x7, waiting for transfers between devices, exchange(): return lax.ppermute(value, 'ctx', [(i, i ^ step) for i in range(ranks)])  7.19 us
    pallas_call x1, Pallas kernels, per_device(): pl.pallas_call(functools.partial(early_kernel, scale, early_steps), out_s...  3.45 us
    pallas_call x1, Pallas kernels, per_device(): pl.pallas_call(functools.partial(late_kernel, scale, gate_scale, early_st...  3.27 us
    pallas_call x1, Pallas kernels, per_device(): pl.pallas_call(functools.partial(gate_kernel, gate_scale), out_shape=(jax...  2.89 us
    unnamed x17, local copies, waits for them, and re-layouts  2.2 us
  transfers between devices with their start and end apart: 7, of which 3 were waited for; matrix products, arithmetic and copies ran while one was open for 0% of the time, Pallas kernels for 7%

profile of v2, /device:TPU:0, one launch (start us, length us, event | category | flops | bytes accessed | tf_op | source)
XLA Modules:
  0.0 47.8 jit_solution(6627465717995883106)
XLA Ops:
  0.6 0.9 %copy.11 = bf16[32,8,2,128]{3,1,2,0:T(8,128)(2,1)S(1)} copy(bf16[32,8,2,128]{3,2,1,0:T(2,128)(2,1)} %bitcast.12) | data formatting | bytes 262144
  1.6 0.0 copy-start
  1.6 3.1 %collective-permute-start = (bf16[256,256]{1,0:T(8,128)(2,1)S(1)}, bf16[256,256]{1,0:T(8,128)(2,1)S(1)}, u32[]{:S(2)}, u32[]{:S(2)}) collective-permute-start(bf16[256,256]{1,0:T(8,128)(2,1)S(1)} %bitcast.7), channel_id=1, source_target_pairs={{0,4},{2,6},{4,0},{6,2},{8,12},{10,14},{12,8},{14,10},{1,5},{3,7},... | collective-permute-start | bytes 393224 | tf_op jit(solution)/shard_map/ppermute | solution.py:262
  4.7 2.6 %collective-permute-start.2 = (bf16[256,256]{1,0:T(8,128)(2,1)S(1)}, bf16[256,256]{1,0:T(8,128)(2,1)S(1)}, u32[]{:S(2)}, u32[]{:S(2)}) collective-permute-start(bf16[256,256]{1,0:T(8,128)(2,1)S(1)} %bitcast.8), channel_id=1, source_target_pairs={{0,8},{2,10},{4,12},{6,14},{8,0},{10,2},{12,4},{14,6},{1,9},{3,11}... | collective-permute-start | bytes 393224 | tf_op jit(solution)/shard_map/ppermute | solution.py:262
  7.2 0.0 collective-permute-start.4
  7.2 1.7 %collective-permute-start.6 = (bf16[256,256]{1,0:T(8,128)(2,1)S(1)}, bf16[256,256]{1,0:T(8,128)(2,1)S(1)}, u32[]{:S(2)}, u32[]{:S(2)}) collective-permute-start(bf16[256,256]{1,0:T(8,128)(2,1)S(1)} %bitcast.10), channel_id=1, source_target_pairs={{0,2},{2,0},{4,6},{6,4},{8,10},{10,8},{12,14},{14,12},{1,3},{3,1},... | collective-permute-start | bytes 393224 | tf_op jit(solution)/shard_map/ppermute | solution.py:262
  9.0 0.7 %collective-permute-done.refs_2_ = bf16[256,256]{1,0:T(8,128)(2,1)S(1)} collective-permute-done((bf16[256,256]{1,0:T(8,128)(2,1)S(1)}, bf16[256,256]{1,0:T(8,128)(2,1)S(1)}, u32[]{:S(2)}, u32[]{:S(2)}) %collective-permute-start) | collective-permute-done | bytes 131104 | tf_op jit(solution)/shard_map/ppermute | solution.py:262
  9.7 0.0 copy-start.1
  9.7 1.7 %collective-permute-start.1 = (bf16[256,256]{1,0:T(8,128)(2,1)S(1)}, bf16[256,256]{1,0:T(8,128)(2,1)S(1)}, u32[]{:S(2)}, u32[]{:S(2)}) collective-permute-start(bf16[256,256]{1,0:T(8,128)(2,1)S(1)} %collective-permute-done.refs_2_), channel_id=1, source_target_pairs={{0,2},{2,0},{4,6},{6,4},{8,10},{10,8},{12,14},{14,12},{1,3},{3,1},... | collective-permute-start | bytes 393224 | tf_op jit(solution)/shard_map/ppermute | solution.py:262
  11.4 6.2 %collective-permute-done.2.refs_3_ = bf16[256,256]{1,0:T(8,128)(2,1)S(1)} collective-permute-done((bf16[256,256]{1,0:T(8,128)(2,1)S(1)}, bf16[256,256]{1,0:T(8,128)(2,1)S(1)}, u32[]{:S(2)}, u32[]{:S(2)}) %collective-permute-start.2) | collective-permute-done | bytes 131104 | tf_op jit(solution)/shard_map/ppermute | solution.py:262
  17.6 0.0 copy-start.2
  17.6 1.5 %collective-permute-start.3 = (bf16[256,256]{1,0:T(8,128)(2,1)S(1)}, bf16[256,256]{1,0:T(8,128)(2,1)S(1)}, u32[]{:S(2)}, u32[]{:S(2)}) collective-permute-start(bf16[256,256]{1,0:T(8,128)(2,1)S(1)} %collective-permute-done.2.refs_3_), channel_id=1, source_target_pairs={{0,2},{2,0},{4,6},{6,4},{8,10},{10,8},{12,14},{14,12},{1,3},{3,1},... | collective-permute-start | bytes 393224 | tf_op jit(solution)/shard_map/ppermute | solution.py:262
  19.1 0.0 collective-permute-done.4.refs_4_
  19.1 0.0 copy-start.3
  19.1 0.5 %collective-permute-start.5 = (bf16[256,256]{1,0:T(8,128)(2,1)S(1)}, bf16[256,256]{1,0:T(8,128)(2,1)S(1)}, u32[]{:S(2)}, u32[]{:S(2)}) collective-permute-start(bf16[256,256]{1,0:T(8,128)(2,1)S(1)} %collective-permute-done.4.refs_4_), channel_id=1, source_target_pairs={{0,2},{2,0},{4,6},{6,4},{8,10},{10,8},{12,14},{14,12},{1,3},{3,1},... | collective-permute-start | bytes 393224 | tf_op jit(solution)/shard_map/ppermute | solution.py:262
  19.6 0.0 collective-permute-done.6.refs_1_
  19.6 0.0 copy-start.4
  19.6 0.0 copy-done
  19.6 0.0 copy-done.1
  19.6 0.0 copy-done.2
  19.6 0.1 copy-done.3
  19.8 0.5 %copy-done.4 = bf16[256,256]{1,0:T(8,128)(2,1)} copy-done((bf16[256,256]{1,0:T(8,128)(2,1)}, bf16[256,256]{1,0:T(8,128)(2,1)S(1)}, u32[]{:S(2)}) %copy-start.4) | copy-done | bytes 131096
  20.3 3.5 %early_key_blocks.1 = (f32[10,5,4,256]{3,2,1,0:T(4,128)}, f32[10,5,4,256]{3,2,1,0:T(4,128)}, f32[2,5,4,384]{3,2,1,0:T(4,128)}, f32[40,128]{1,0:T(8,128)}, f32[40,128]{1,0:T(8,128)}) custom-call(s32[4]{0:T(128)} %lengths_ref.3, bf16[10,256,128]{2,1,0:T(8,128)(2,1)} %bitcast.5, bf16[10,128,128]{2,1,0:T(8,128)(2,1)} %wq_ref.3, bf16[256,256]{1,0:T(8,128)(2,1)} %bitcast.11, ...), custom_call_target="tpu_custom_call" | custom-call | tf_op jit(solution)/shard_map/early_key_blocks/pallas_call | solution.py:276
  23.7 0.0 collective-permute-done.1.refs_0_
  23.7 0.0 copy-start.5
  23.7 0.0 collective-permute-done.3.refs_1_
  23.7 0.0 copy-start.6
  23.7 0.3 collective-permute-done.5.refs_2_
  24.1 0.0 copy-start.7
  24.1 0.3 copy-done.5
  24.4 0.0 copy-done.6
  24.4 0.3 copy-done.7
  24.7 3.3 %late_key_blocks.1 = (f32[10,4,32]{2,1,0:T(4,128)}, bf16[8,80,128]{2,1,0:T(8,128)(2,1)}, bf16[2,32,384]{2,1,0:T(8,128)(2,1)}, f32[2,32,128]{2,1,0:T(8,128)}) custom-call(s32[4]{0:T(128)} %lengths_ref.3, bf16[10,256,128]{2,1,0:T(8,128)(2,1)} %bitcast.6, bf16[2,384,128]{2,1,0:T(8,128)(2,1)} %wk_ref.1, bf16[256,256]{1,0:T(8,128)(2,1)} %copy-done.5, ...), custom_call_target="tpu_custom_call" | custom-call | tf_op jit(solution)/shard_map/late_key_blocks/pallas_call | solution.py:291
  28.0 16.9 %all_to_all.5.packed_ref = bf16[8,80,128]{2,1,0:T(8,128)(2,1)} all-to-all(bf16[8,80,128]{2,1,0:T(8,128)(2,1)} %get-tuple-element.22), channel_id=1, replica_groups=mesh['groups'=2,'ctx'=8,'head'=2] {'ctx'}, dimensions={0} | all-to-all | bytes 327680 | tf_op jit(solution)/shard_map/all_to_all | solution.py:311
  44.9 2.9 %gate_gradients.1 = (f32[4,2,128]{2,1,0:T(2,128)}, f32[10,128,128]{2,1,0:T(8,128)}, f32[2,384,128]{2,1,0:T(8,128)}) custom-call(bf16[8,80,128]{2,1,0:T(8,128)(2,1)} %all_to_all.5.packed_ref, bf16[2,32,384]{2,1,0:T(8,128)(2,1)} %get-tuple-element.23.pooled_k_ref, f32[2,32,128]{2,1,0:T(8,128)} %get-tuple-element.24.key_proj_ref, bf16[10,128,128]{2,1,0:T(8,128)(2,1)} %wq_ref.3), custom_call_target="tpu_custom_call" | custom-call | tf_op jit(solution)/shard_map/gate_gradients/pallas_call | solution.py:312
Async XLA Ops:
  1.6 18.1 %copy-start = (bf16[32,8,2,128]{3,1,2,0:T(8,128)(2,1)}, bf16[32,8,2,128]{3,1,2,0:T(8,128)(2,1)S(1)}, u32[]{:S(2)}) copy-start(bf16[32,8,2,128]{3,1,2,0:T(8,128)(2,1)S(1)} %copy.11) | copy-start | bytes 393220
  1.6 8.1 %collective-permute-start = (bf16[256,256]{1,0:T(8,128)(2,1)S(1)}, bf16[256,256]{1,0:T(8,128)(2,1)S(1)}, u32[]{:S(2)}, u32[]{:S(2)}) collective-permute-start(bf16[256,256]{1,0:T(8,128)(2,1)S(1)} %bitcast.7), channel_id=1, source_target_pairs={{0,4},{2,6},{4,0},{6,2},{8,12},{10,14},{12,8},{14,10},{1,5},{3,7},... | collective-permute-start | bytes 393224 | tf_op jit(solution)/shard_map/ppermute | solution.py:262
  4.7 12.9 %collective-permute-start.2 = (bf16[256,256]{1,0:T(8,128)(2,1)S(1)}, bf16[256,256]{1,0:T(8,128)(2,1)S(1)}, u32[]{:S(2)}, u32[]{:S(2)}) collective-permute-start(bf16[256,256]{1,0:T(8,128)(2,1)S(1)} %bitcast.8), channel_id=1, source_target_pairs={{0,8},{2,10},{4,12},{6,14},{8,0},{10,2},{12,4},{14,6},{1,9},{3,11}... | collective-permute-start | bytes 393224 | tf_op jit(solution)/shard_map/ppermute | solution.py:262
  7.2 11.9 %collective-permute-start.4 = (bf16[256,256]{1,0:T(8,128)(2,1)S(1)}, bf16[256,256]{1,0:T(8,128)(2,1)S(1)}, u32[]{:S(2)}, u32[]{:S(2)}) collective-permute-start(bf16[256,256]{1,0:T(8,128)(2,1)S(1)} %bitcast.9), channel_id=1, source_target_pairs={{0,12},{2,14},{4,8},{6,10},{8,4},{10,6},{12,0},{14,2},{1,13},{3,15... | collective-permute-start | bytes 393224 | tf_op jit(solution)/shard_map/ppermute | solution.py:262
  7.2 12.4 %collective-permute-start.6 = (bf16[256,256]{1,0:T(8,128)(2,1)S(1)}, bf16[256,256]{1,0:T(8,128)(2,1)S(1)}, u32[]{:S(2)}, u32[]{:S(2)}) collective-permute-start(bf16[256,256]{1,0:T(8,128)(2,1)S(1)} %bitcast.10), channel_id=1, source_target_pairs={{0,2},{2,0},{4,6},{6,4},{8,10},{10,8},{12,14},{14,12},{1,3},{3,1},... | collective-permute-start | bytes 393224 | tf_op jit(solution)/shard_map/ppermute | solution.py:262
  9.7 9.9 %copy-start.1 = (bf16[256,256]{1,0:T(8,128)(2,1)}, bf16[256,256]{1,0:T(8,128)(2,1)S(1)}, u32[]{:S(2)}) copy-start(bf16[256,256]{1,0:T(8,128)(2,1)S(1)} %collective-permute-done.refs_2_) | copy-start | bytes 393220
  9.7 14.0 %collective-permute-start.1 = (bf16[256,256]{1,0:T(8,128)(2,1)S(1)}, bf16[256,256]{1,0:T(8,128)(2,1)S(1)}, u32[]{:S(2)}, u32[]{:S(2)}) collective-permute-start(bf16[256,256]{1,0:T(8,128)(2,1)S(1)} %collective-permute-done.refs_2_), channel_id=1, source_target_pairs={{0,2},{2,0},{4,6},{6,4},{8,10},{10,8},{12,14},{14,12},{1,3},{3,1},... | collective-permute-start | bytes 393224 | tf_op jit(solution)/shard_map/ppermute | solution.py:262
  17.6 2.0 %copy-start.2 = (bf16[256,256]{1,0:T(8,128)(2,1)}, bf16[256,256]{1,0:T(8,128)(2,1)S(1)}, u32[]{:S(2)}) copy-start(bf16[256,256]{1,0:T(8,128)(2,1)S(1)} %collective-permute-done.2.refs_3_) | copy-start | bytes 393220
  17.6 6.1 %collective-permute-start.3 = (bf16[256,256]{1,0:T(8,128)(2,1)S(1)}, bf16[256,256]{1,0:T(8,128)(2,1)S(1)}, u32[]{:S(2)}, u32[]{:S(2)}) collective-permute-start(bf16[256,256]{1,0:T(8,128)(2,1)S(1)} %collective-permute-done.2.refs_3_), channel_id=1, source_target_pairs={{0,2},{2,0},{4,6},{6,4},{8,10},{10,8},{12,14},{14,12},{1,3},{3,1},... | collective-permute-start | bytes 393224 | tf_op jit(solution)/shard_map/ppermute | solution.py:262
  19.1 0.7 %copy-start.3 = (bf16[256,256]{1,0:T(8,128)(2,1)}, bf16[256,256]{1,0:T(8,128)(2,1)S(1)}, u32[]{:S(2)}) copy-start(bf16[256,256]{1,0:T(8,128)(2,1)S(1)} %collective-permute-done.4.refs_4_) | copy-start | bytes 393220
  19.1 5.0 %collective-permute-start.5 = (bf16[256,256]{1,0:T(8,128)(2,1)S(1)}, bf16[256,256]{1,0:T(8,128)(2,1)S(1)}, u32[]{:S(2)}, u32[]{:S(2)}) collective-permute-start(bf16[256,256]{1,0:T(8,128)(2,1)S(1)} %collective-permute-done.4.refs_4_), channel_id=1, source_target_pairs={{0,2},{2,0},{4,6},{6,4},{8,10},{10,8},{12,14},{14,12},{1,3},{3,1},... | collective-permute-start | bytes 393224 | tf_op jit(solution)/shard_map/ppermute | solution.py:262
  19.6 0.6 %copy-start.4 = (bf16[256,256]{1,0:T(8,128)(2,1)}, bf16[256,256]{1,0:T(8,128)(2,1)S(1)}, u32[]{:S(2)}) copy-start(bf16[256,256]{1,0:T(8,128)(2,1)S(1)} %collective-permute-done.6.refs_1_) | copy-start | bytes 393220
  23.7 0.6 %copy-start.5 = (bf16[256,256]{1,0:T(8,128)(2,1)}, bf16[256,256]{1,0:T(8,128)(2,1)S(1)}, u32[]{:S(2)}) copy-start(bf16[256,256]{1,0:T(8,128)(2,1)S(1)} %collective-permute-done.1.refs_0_) | copy-start | bytes 393220
  23.7 0.7 %copy-start.6 = (bf16[256,256]{1,0:T(8,128)(2,1)}, bf16[256,256]{1,0:T(8,128)(2,1)S(1)}, u32[]{:S(2)}) copy-start(bf16[256,256]{1,0:T(8,128)(2,1)S(1)} %collective-permute-done.3.refs_1_) | copy-start | bytes 393220
  24.1 0.6 %copy-start.7 = (bf16[256,256]{1,0:T(8,128)(2,1)}, bf16[256,256]{1,0:T(8,128)(2,1)S(1)}, u32[]{:S(2)}) copy-start(bf16[256,256]{1,0:T(8,128)(2,1)S(1)} %collective-permute-done.5.refs_2_) | copy-start | bytes 393220
